TPU v7x, 32 devices: a whole 2x2x4 slice. The times are simulated.
32 devices in a mesh: expert: 4 (over y, x), dp: 4 (over z), tensor: 2 (over core).
Axes of the slice: x: 2, y: 2, z: 4, core: 2. Of those that a mesh axis runs over, the one named last changes fastest.
Arguments:
- tokens: bfloat16 [16384, 768], P(('expert', 'dp')), may hold values from -6 to 6
- lengths: int32 [16, 4], P(('expert', 'dp')), may hold values from 1 to 768, 1024 in all within a row
- routes: int32 [16384, 1], P(('expert', 'dp')), may hold values from 0 to 7; in each aligned block of 1024 rows (0 to 1023, 1024 to 2047, ...) at most 256 rows name the same one
- cotangent: bfloat16 [16384, 768], P(('expert', 'dp')), may hold values from -6 to 6
- norm_gains: float32 [2, 768], replicated, may hold values from 0.5 to 1.5
- attn_biases: float32 [3, 768], replicated, may hold values from -1.75 to 1.75
- w_attn: float32 [3, 768, 768], P(None, None, 'tensor'), may hold values from -0.3125 to 0.3125
- w_proj: float32 [768, 768], P('tensor'), may hold values from -0.625 to 0.625
- w_router: float32 [768, 8], replicated, may hold values from -0.109375 to 0.109375
- w_in: float32 [8, 768, 3072], P('expert', 'dp', 'tensor'), may hold values from -0.21875 to 0.21875
- w_out: float32 [8, 768, 3072], P('expert', 'dp', 'tensor'), may hold values from -2.5 to 2.5
- gains_moment: float32 [2, 768], replicated, may hold values from -160 to 160
- biases_moment: float32 [3, 768], replicated, may hold values from -160 to 160
- attn_moment: float32 [3, 768, 768], P(None, None, 'tensor'), may hold values from -1024 to 1024
- proj_moment: float32 [768, 768], P('tensor'), may hold values from -320 to 320
- router_moment: float32 [768, 8], replicated, may hold values from -32768 to 32768
- in_moment: float32 [8, 768, 3072], P('expert', 'dp', 'tensor'), may hold values from -224 to 224
- out_moment: float32 [8, 768, 3072], P('expert', 'dp', 'tensor'), may hold values from -20 to 20
Outputs:
- layer_out: bfloat16 [16384, 768], P(('expert', 'dp'))
- input_grad: float32 [16384, 768], P(('expert', 'dp'))
- expert_branch: float32 [16384, 768], P(('expert', 'dp'))
- updated_norm_gains: float32 [2, 768], replicated
- new_gains_moment: float32 [2, 768], replicated
- new_biases: float32 [3, 768], replicated
- new_biases_moment: float32 [3, 768], replicated
- new_attn: float32 [3, 768, 768], P(None, None, 'tensor')
- new_attn_moment: float32 [3, 768, 768], P(None, None, 'tensor')
- new_proj: float32 [768, 768], P('tensor')
- new_proj_moment: float32 [768, 768], P('tensor')
- new_router: float32 [768, 8], replicated
- new_router_moment: float32 [768, 8], replicated
- new_in: float32 [8, 768, 3072], P('expert', 'dp', 'tensor')
- new_in_moment: float32 [8, 768, 3072], P('expert', 'dp', 'tensor')
- new_out: float32 [8, 768, 3072], P('expert', 'dp', 'tensor')
- new_out_moment: float32 [8, 768, 3072], P('expert', 'dp', 'tensor')
Inputs may be any that keep to these rules, and one draw needn't show every extreme that they name: `routes`: within each data group (aligned blocks of 1024 rows) no expert is named by more than 256 tokens, and in some groups one expert is named by exactly 256. Row g holds the lengths of the 4 sequences of data group g in the order in which they lie; they sum to 1024 and the largest is 768.
All inputs are finite; a program needn't handle non-finite values.
Results may differ from a plain program's by a relative error of at most 0.025.
The roundings to bfloat16 on the way count: a program that leaves them out, or rounds other values in their place, can miss the bound.
Values may be sent and summed in bfloat16 or wider, within the bound.
A program may use at most 256 MiB of HBM per device.

v0:
```python
import math

import jax
import jax.numpy as jnp
from jax import lax
from jax.sharding import PartitionSpec as P

HD = 64
FF = 3072
NS_STEPS = 5


PRECISE = lax.Precision.HIGHEST
MOMENT = 0.95
VECTOR_DECAY = 0.9
VECTOR_RATE = 0.2
COEF_A = 3.4445
COEF_B = -4.775
COEF_C = 2.0315
RATE_ATTN = 0.05
RATE_PROJ = 0.1
RATE_ROUTER = 0.03
RATE_IN = 0.04
RATE_OUT = 0.4


def rms_norm(values, gain_row):
    factor = lax.rsqrt(jnp.mean(values * values, axis=-1, keepdims=True) + 1e-06)
    return values * factor * gain_row


def newton_whole(update):
    frobenius = jnp.sqrt(jnp.sum(update * update, axis=(-2, -1), keepdims=True))
    orthogonal = update / (frobenius + 1e-07)
    for iteration in range(NS_STEPS):
        gram_matrix = jnp.einsum("kif,kjf->kij", orthogonal, orthogonal, precision=PRECISE)
        polynomial = COEF_B * gram_matrix + COEF_C * jnp.einsum(
            "kij,kjl->kil", gram_matrix, gram_matrix, precision=PRECISE
        )
        orthogonal = COEF_A * orthogonal + jnp.einsum(
            "kij,kjf->kif", polynomial, orthogonal, precision=PRECISE
        )
    return orthogonal


def vector_step(param_rows, moment, gradient):
    moment_new = VECTOR_DECAY * moment + (1.0 - VECTOR_DECAY) * gradient
    pieces = moment_new.reshape(moment_new.shape[0], -1, HD)
    magnitude = jnp.sqrt(jnp.mean(pieces * pieces, axis=-1, keepdims=True) + 1e-06)
    return (param_rows - VECTOR_RATE * (pieces / magnitude).reshape(moment_new.shape), moment_new)


def body(
    tokens,
    lengths,
    routes,
    cotangent,
    norm_gains,
    attn_biases,
    w_attn,
    w_proj,
    w_router,
    w_in,
    w_out,
    gains_moment,
    biases_moment,
    attn_moment,
    proj_moment,
    router_moment,
    in_moment,
    out_moment,
):
    row_count, model_width = tokens.shape
    tensor_count = lax.axis_size("tensor")
    expert_count = lax.axis_size("expert")
    data_count = lax.axis_size("dp")
    tensor_index = lax.axis_index("tensor")
    head_width = w_attn.shape[2]
    local_heads = head_width // HD
    expert_local = w_in.shape[0]
    expert_total = expert_local * expert_count
    capacity = 2 * row_count // expert_total
    block_rows = min(512, row_count)
    block_count = row_count // block_rows
    head_scale = HD ** (-0.5)
    in_low, out_low = (
        lax.all_gather(w_in.astype(jnp.bfloat16), "dp", axis=1, tiled=True),
        lax.all_gather(w_out.astype(jnp.bfloat16), "dp", axis=1, tiled=True),
    )
    seq_ends = jnp.cumsum(lengths[0])
    position = jnp.arange(row_count, dtype=jnp.int32)
    segment = jnp.sum((position[:, None] >= seq_ends[None, :]).astype(jnp.int32), axis=1)
    route_ids = routes[:, 0]
    chosen_int = (route_ids[:, None] == jnp.arange(expert_total, dtype=jnp.int32)[None, :]).astype(
        jnp.int32
    )
    slot_ids = jnp.sum((jnp.cumsum(chosen_int, axis=0) - 1) * chosen_int, axis=1)
    target = (
        route_ids % expert_local * expert_count + route_ids // expert_local
    ) * capacity + slot_ids

    def spread(values):
        return lax.all_gather(values, "tensor", axis=3, tiled=True)

    def dispatch(values_low):
        flat_rows = (
            jnp.zeros((expert_total * capacity, model_width), jnp.bfloat16)
            .at[target]
            .set(values_low)
        )
        grid_rows = flat_rows.reshape(expert_local, expert_count, capacity, model_width)
        arrived = lax.all_to_all(grid_rows, "expert", split_axis=1, concat_axis=1, tiled=True)
        return arrived.reshape(expert_local, expert_count * capacity, model_width)

    def give_back(values):
        grid_rows = values.reshape(expert_local, expert_count, capacity, model_width)
        summed = lax.psum_scatter(
            grid_rows.astype(jnp.bfloat16), "tensor", scatter_dimension=3, tiled=True
        )
        arrived = lax.all_to_all(summed, "expert", split_axis=1, concat_axis=1, tiled=True)
        return spread(arrived).reshape(expert_total * capacity, model_width)[target]

    x_float = tokens.astype(jnp.float32)
    normed, norm_back = jax.vjp(rms_norm, x_float, norm_gains[0])
    normalized_reduced = normed.astype(jnp.bfloat16)
    attention_reduced = w_attn.astype(jnp.bfloat16)
    own_bias = lax.dynamic_slice_in_dim(attn_biases[:2], tensor_index * head_width, head_width, 1)
    projected_output = jnp.einsum(
        "kj,bjc->bkc", normalized_reduced, attention_reduced, preferred_element_type=jnp.float32
    )
    query_low = (projected_output[0] + own_bias[0]).astype(jnp.bfloat16)
    key_low = projected_output[1].astype(jnp.bfloat16)
    value_low = (projected_output[2] + own_bias[1]).astype(jnp.bfloat16)
    key_heads = key_low.reshape(row_count, local_heads, HD)
    value_heads = value_low.reshape(row_count, local_heads, HD)
    query_blocks = query_low.reshape(block_count, block_rows, local_heads, HD)
    segment_blocks = segment.reshape(block_count, block_rows)

    def block_scores(query_block, segment_block):
        raw_scores = (
            jnp.einsum("qhd,khd->hqk", query_block, key_heads, preferred_element_type=jnp.float32)
            * head_scale
        )
        same_seq = segment_block[:, None] == segment[None, :]
        return jnp.where(same_seq[None], raw_scores, -1e30)

    def forward_block(pieces):
        query_block, segment_block = pieces
        scores = block_scores(query_block, segment_block)
        weights = jax.nn.softmax(scores, axis=-1)
        log_total = jax.nn.logsumexp(scores, axis=-1)
        heads_part = jnp.einsum(
            "hqk,khd->qhd",
            weights.astype(jnp.bfloat16),
            value_heads,
            preferred_element_type=jnp.float32,
        )
        return (heads_part.astype(jnp.bfloat16), log_total)

    head_blocks, log_totals = lax.map(forward_block, (query_blocks, segment_blocks))
    heads_low = head_blocks.reshape(row_count, head_width)
    proj_low = w_proj.astype(jnp.bfloat16)
    attn_part = jnp.dot(heads_low, proj_low, preferred_element_type=jnp.float32)
    attn_full = lax.psum(attn_part, "tensor")
    hidden = x_float + attn_full + attn_biases[2]
    routed, routed_back = jax.vjp(rms_norm, hidden, norm_gains[1])
    routed_low = routed.astype(jnp.bfloat16)
    router_low = w_router.astype(jnp.bfloat16)
    logits = jnp.dot(routed_low, router_low, preferred_element_type=jnp.float32)
    chosen = chosen_int.astype(jnp.float32)

    def gate_of(logit_rows):
        return jnp.sum(jax.nn.softmax(logit_rows, axis=-1) * chosen, axis=-1, keepdims=True)

    gate_value, gate_back = jax.vjp(gate_of, logits)
    expert_rows = dispatch(routed_low)
    preact = jnp.einsum("jrd,jdf->jrf", expert_rows, in_low, preferred_element_type=jnp.float32)
    activation, gelu_back = jax.vjp(jax.nn.gelu, preact)
    act_low = activation.astype(jnp.bfloat16)
    expert_part = jnp.einsum("jrf,jdf->jrd", act_low, out_low, preferred_element_type=jnp.float32)
    picked = give_back(expert_part).astype(jnp.float32)
    expert_branch = gate_value * picked
    layer_out = (hidden + expert_branch).astype(jnp.bfloat16)
    grad_rows = cotangent.astype(jnp.float32)
    back_gate = jnp.sum(grad_rows * picked, axis=1, keepdims=True)
    back_logits = gate_back(back_gate)[0]
    back_picked = (gate_value * grad_rows).astype(jnp.bfloat16)
    back_expert = dispatch(back_picked)
    back_act = jnp.einsum("jrd,jdf->jrf", back_expert, out_low, preferred_element_type=jnp.float32)
    back_preact = gelu_back(back_act)[0].astype(jnp.bfloat16)
    grad_out_w = jnp.einsum(
        "jrd,jrf->jdf", back_expert, act_low, preferred_element_type=jnp.float32
    )
    grad_in_w = jnp.einsum(
        "jrd,jrf->jdf", expert_rows, back_preact, preferred_element_type=jnp.float32
    )
    back_rows = jnp.einsum("jrf,jdf->jrd", back_preact, in_low, preferred_element_type=jnp.float32)
    back_routed = give_back(back_rows).astype(jnp.float32) + jnp.dot(
        back_logits, router_low.astype(jnp.float32).T, precision=PRECISE
    )
    grad_router = jnp.dot(routed_low.astype(jnp.float32).T, back_logits, precision=PRECISE)
    hidden_norm_grad, grad_gain_two = routed_back(back_routed)
    hidden_grad = grad_rows + hidden_norm_grad
    grad_bias_out = jnp.sum(hidden_grad, axis=0)
    hidden_grad_low = hidden_grad.astype(jnp.bfloat16)
    grad_proj = jnp.einsum(
        "rf,rd->fd", heads_low, hidden_grad_low, preferred_element_type=jnp.float32
    )
    heads_grad_low = jnp.einsum(
        "rd,fd->rf", hidden_grad_low, proj_low, preferred_element_type=jnp.float32
    ).astype(jnp.bfloat16)
    heads_grad_blocks = heads_grad_low.reshape(block_count, block_rows, local_heads, HD)

    def backward_block(carry, pieces):
        key_acc, value_acc = carry
        query_block, segment_block, grad_block, log_total = pieces
        scores = block_scores(query_block, segment_block)
        weights = jnp.exp(scores - log_total[:, :, None])
        value_acc = value_acc + jnp.einsum(
            "hqk,qhd->khd",
            weights.astype(jnp.bfloat16),
            grad_block,
            preferred_element_type=jnp.float32,
        )
        grad_weights = jnp.einsum(
            "qhd,khd->hqk", grad_block, value_heads, preferred_element_type=jnp.float32
        )
        grad_scores = (
            weights * (grad_weights - jnp.sum(grad_weights * weights, axis=-1, keepdims=True))
        ).astype(jnp.bfloat16)
        grad_query = (
            jnp.einsum("hqk,khd->qhd", grad_scores, key_heads, preferred_element_type=jnp.float32)
            * head_scale
        )
        key_acc = (
            key_acc
            + jnp.einsum(
                "hqk,qhd->khd", grad_scores, query_block, preferred_element_type=jnp.float32
            )
            * head_scale
        )
        return ((key_acc, value_acc), grad_query.astype(jnp.bfloat16))

    zero_heads = jnp.zeros((row_count, local_heads, HD), jnp.float32)
    (key_total, value_total), query_grads = lax.scan(
        backward_block,
        (zero_heads, zero_heads),
        (query_blocks, segment_blocks, heads_grad_blocks, log_totals),
    )
    query_grad = query_grads.reshape(row_count, head_width)
    key_grad = key_total.reshape(row_count, head_width).astype(jnp.bfloat16)
    value_grad = value_total.reshape(row_count, head_width).astype(jnp.bfloat16)
    query_key_value_gradient = jnp.stack([query_grad, key_grad, value_grad])
    attention_gradient = jnp.einsum(
        "gy,egz->eyz",
        normalized_reduced,
        query_key_value_gradient,
        preferred_element_type=jnp.float32,
    )
    normalized_gradient = jnp.einsum(
        "txp,tgp->xg",
        query_key_value_gradient,
        attention_reduced,
        preferred_element_type=jnp.float32,
    )
    own_bias_grad = jnp.stack(
        [
            jnp.sum(query_grad, axis=0, dtype=jnp.float32),
            jnp.sum(value_grad, axis=0, dtype=jnp.float32),
        ]
    )
    bias_padded = lax.dynamic_update_slice_in_dim(
        jnp.zeros((2, model_width), jnp.float32), own_bias_grad, tensor_index * head_width, 1
    )
    normalized_gradient, bias_pair = (
        lax.psum(normalized_gradient.astype(jnp.bfloat16), "tensor").astype(jnp.float32),
        lax.psum(bias_padded.astype(jnp.bfloat16), "tensor").astype(jnp.float32),
    )
    input_norm_grad, grad_gain_one = norm_back(normalized_gradient)
    input_grad = hidden_grad + input_norm_grad
    gain_grads = jnp.stack([grad_gain_one, grad_gain_two])
    bias_grads = jnp.stack([bias_pair[0], bias_pair[1], grad_bias_out])
    attention_gradient, grad_proj, grad_router, gain_grads, bias_grads = lax.psum(
        (attention_gradient, grad_proj, grad_router, gain_grads, bias_grads), ("expert", "dp")
    )
    grad_in_w, grad_out_w = (
        lax.psum_scatter(
            grad_in_w.astype(jnp.bfloat16), "dp", scatter_dimension=1, tiled=True
        ).astype(jnp.float32),
        lax.psum_scatter(
            grad_out_w.astype(jnp.bfloat16), "dp", scatter_dimension=1, tiled=True
        ).astype(jnp.float32),
    )
    updated_norm_gains, new_gains_moment = vector_step(norm_gains, gains_moment, gain_grads)
    new_biases, new_biases_moment = vector_step(attn_biases, biases_moment, bias_grads)
    attn_moment_new = MOMENT * attn_moment + attention_gradient
    attn_update = attention_gradient + MOMENT * attn_moment_new
    proj_moment_new = MOMENT * proj_moment + grad_proj
    proj_update = grad_proj + MOMENT * proj_moment_new
    dense_stack = jnp.concatenate([attn_update, proj_update.T[None]], axis=0)
    owned = lax.all_to_all(dense_stack, "tensor", split_axis=0, concat_axis=2, tiled=True)
    settled = lax.all_to_all(
        newton_whole(owned).astype(jnp.bfloat16), "tensor", split_axis=2, concat_axis=0, tiled=True
    ).astype(jnp.float32)
    dense_factor = math.sqrt(model_width)
    new_attn = w_attn - RATE_ATTN * dense_factor * settled[:3]
    new_proj = w_proj - RATE_PROJ * dense_factor * settled[3].T
    router_moment_new = MOMENT * router_moment + grad_router
    router_update = grad_router + MOMENT * router_moment_new
    router_ortho = newton_whole(router_update.T[None])[0].T
    new_router = w_router - RATE_ROUTER * math.sqrt(max(model_width, expert_total)) * router_ortho
    in_moment_new = MOMENT * in_moment + grad_in_w
    in_update = grad_in_w + MOMENT * in_moment_new
    out_moment_new = MOMENT * out_moment + grad_out_w
    out_update = grad_out_w + MOMENT * out_moment_new
    expert_stack = jnp.concatenate([in_update, out_update], axis=0)
    stack_count, row_part, col_part = expert_stack.shape
    slot_total = data_count * tensor_count
    filler = jnp.zeros((slot_total - stack_count, row_part, col_part), jnp.float32)
    padded = jnp.concatenate([expert_stack, filler], axis=0).reshape(
        data_count, tensor_count, row_part, col_part
    )
    whole_matrix = lax.all_to_all(
        lax.all_to_all(padded.astype(jnp.bfloat16), "dp", split_axis=0, concat_axis=2, tiled=True),
        "tensor",
        split_axis=1,
        concat_axis=3,
        tiled=True,
    ).astype(padded.dtype)
    whole_ortho = newton_whole(whole_matrix.reshape(1, model_width, tensor_count * col_part))
    returned = lax.all_to_all(
        lax.all_to_all(
            whole_ortho.reshape(1, 1, model_width, tensor_count * col_part).astype(jnp.bfloat16),
            "dp",
            split_axis=2,
            concat_axis=0,
            tiled=True,
        ),
        "tensor",
        split_axis=3,
        concat_axis=1,
        tiled=True,
    ).astype(jnp.float32)
    expert_ortho = returned.reshape(slot_total, row_part, col_part)[:stack_count]
    expert_factor = math.sqrt(max(model_width, FF))
    new_in = w_in - RATE_IN * expert_factor * expert_ortho[:expert_local]
    new_out = w_out - RATE_OUT * expert_factor * expert_ortho[expert_local:]
    return (
        layer_out,
        input_grad,
        expert_branch,
        updated_norm_gains,
        new_gains_moment,
        new_biases,
        new_biases_moment,
        new_attn,
        attn_moment_new,
        new_proj,
        proj_moment_new,
        new_router,
        router_moment_new,
        new_in,
        in_moment_new,
        new_out,
        out_moment_new,
    )


def solution(mesh):
    return jax.shard_map(
        body,
        mesh=mesh,
        in_specs=(
            P(("expert", "dp"), None),
            P(("expert", "dp"), None),
            P(("expert", "dp"), None),
            P(("expert", "dp"), None),
            P(),
            P(),
            P(None, None, "tensor"),
            P("tensor", None),
            P(),
            P("expert", "dp", "tensor"),
            P("expert", "dp", "tensor"),
            P(),
            P(),
            P(None, None, "tensor"),
            P("tensor", None),
            P(),
            P("expert", "dp", "tensor"),
            P("expert", "dp", "tensor"),
        ),
        out_specs=(
            P(("expert", "dp"), None),
            P(("expert", "dp"), None),
            P(("expert", "dp"), None),
            P(),
            P(),
            P(),
            P(),
            P(None, None, "tensor"),
            P(None, None, "tensor"),
            P("tensor", None),
            P("tensor", None),
            P(),
            P(),
            P("expert", "dp", "tensor"),
            P("expert", "dp", "tensor"),
            P("expert", "dp", "tensor"),
            P("expert", "dp", "tensor"),
        ),
        check_vma=False,
    )
```

profile of v0, /device:TPU:0, one launch (start us, length us, event | category | flops | bytes accessed | tf_op | source)
XLA Modules:
  0.0 1671.9 jit_solution(17689428208559745661)
XLA Ops:
  23.4 25.5 %while.27 = (s32[]{:T(128)}, bf16[2,512,6,64]{1,3,2,0:T(8,128)(2,1)S(1)}, f32[2,6,512]{2,1,0:T(8,128)S(1)}, s32[2,512]{1,0:T(2,128)S(1)}, s32[1024]{0:T(1024)S(1...) while((s32[]{:T(128)}, ...), condition=%wide.region_7.8_spmd, body=%wide.region_3.7_spmd.sunk | while | flops 850076672 | bytes 42383476 | solution.py:160
  61.9 17.3 %all-reduce.6.cloned.1.call-done = f32[1024,768]{1,0:T(8,128)} async-done(((f32[1024,768]{1,0:T(8,128)}), f32[1024,768]{1,0:T(8,128)}) %all-reduce.6.cloned.1.call-update) | async-done | bytes 3145744 | tf_op jit(solution)/shard_map/psum | solution.py:164
  94.3 40.8 %all_to_all.95 = bf16[2,4,256,768]{3,2,0,1:T(8,128)(2,1)S(1)} all-to-all(bf16[2,4,256,768]{3,2,0,1:T(8,128)(2,1)S(1)} %copy.195), channel_id=1, replica_groups=mesh['expert'=4,'dp'=4,'tensor'=2] {'expert'}, dimensions={1} | all-to-all | bytes 6291456 | tf_op jit(solution)/shard_map/all_to_all | solution.py:112
  158.8 79.1 %all-gather.7.cloned.1.call-done = bf16[2,768,1536]{2,1,0:T(8,128)(2,1)} async-done(((bf16[2,192,1536]{2,1,0:T(8,128)(2,1)}), bf16[2,768,1536]{2,1,0:T(8,128)(2,1)}) %all-gather.7.cloned.1.call-update) | async-done | bytes 4718608 | tf_op jit(solution)/shard_map/all_gather | solution.py:88
  278.7 24.9 %all_to_all.96 = bf16[2,4,256,384]{3,2,0,1:T(8,128)(2,1)} all-to-all(bf16[2,4,256,384]{3,2,0,1:T(8,128)(2,1)} %copy.197), channel_id=1, replica_groups=mesh['expert'=4,'dp'=4,'tensor'=2] {'expert'}, dimensions={1} | all-to-all | bytes 3145728 | tf_op jit(solution)/shard_map/all_to_all | solution.py:120
  340.0 41.1 %all_to_all.97 = bf16[2,4,256,768]{3,2,0,1:T(8,128)(2,1)S(1)} all-to-all(bf16[2,4,256,768]{3,2,0,1:T(8,128)(2,1)S(1)} %copy.199), channel_id=1, replica_groups=mesh['expert'=4,'dp'=4,'tensor'=2] {'expert'}, dimensions={1} | all-to-all | bytes 6291456 | tf_op jit(solution)/shard_map/all_to_all | solution.py:112
  438.0 24.9 %all_to_all.98 = bf16[2,4,256,384]{3,2,0,1:T(8,128)(2,1)} all-to-all(bf16[2,4,256,384]{3,2,0,1:T(8,128)(2,1)} %copy.201), channel_id=1, replica_groups=mesh['expert'=4,'dp'=4,'tensor'=2] {'expert'}, dimensions={1} | all-to-all | bytes 3145728 | tf_op jit(solution)/shard_map/all_to_all | solution.py:120
  514.2 54.3 %while.28 = (s32[]{:T(128)}, f32[1024,6,64]{0,2,1:T(8,128)}, f32[1024,6,64]{0,2,1:T(8,128)}, bf16[2,512,6,64]{1,3,2,0:T(8,128)(2,1)}, bf16[2,512,6,64]{1,3,2,0:T...) while((s32[]{:T(128)}, f32[1024,6,64]{0,2,1:T(8,128)}, ...), condition=%wide.region_25.26_spmd.clone, body=%wide.region_23.25_spmd.clone.sunk | while | flops 2063332352 | bytes 141789456 | solution.py:245
  606.6 54.4 %reduce-scatter.9.cloned.1.call-done = bf16[2,192,1536]{2,1,0:T(8,128)(2,1)} async-done(((bf16[2,768,1536]{2,1,0:T(8,128)(2,1)}), bf16[2,192,1536]{2,1,0:T(8,128)(2,1)}) %reduce-scatter.9.cloned.1.call-update) | async-done | bytes 1179664 | tf_op jit(solution)/shard_map/reduce_scatter | solution.py:287
  676.1 78.9 %all-reduce = (f32[2,768]{1,0:T(2,128)}, f32[3,768]{1,0:T(4,128)}, f32[768,8]{0,1:T(8,128)}) all-reduce(f32[2,768]{1,0:T(2,128)} %pad_maximum_fusion.5, f32[3,768]{1,0:T(4,128)S(1)} %pad_maximum_fusion.4, f32[768,8]{0,1:T(8,128)} %fusion.210), channel_id=1, replica_groups=mesh['expert'=4,'dp'=4,'tensor'=2] {'expert','dp'}, use_global_device_ids=true, to_apply=%region_30.31 | all-reduce | flops 9984 | bytes 79872 | tf_op jit(solution)/shard_map/psum | solution.py:283
  757.8 62.0 %all-reduce.10.cloned.1.call-done = (f32[384,768]{1,0:T(8,128)}, f32[3,768,384]{1,2,0:T(8,128)}) async-done(((f32[384,768]{1,0:T(8,128)}, f32[3,768,384]{1,2,0:T(8,128)}), (f32[384,768]{1,0:T(8,128)}, f32[3,768,384]{1,2,0:T(8,128)})) %all-reduce.10.cloned.1.call-update) | async-done | bytes 4718608 | tf_op jit(solution)/shard_map/psum | solution.py:283
  1077.6 25.9 %fusion.47 = f32[768,768,1]{1,0,2:T(8,128)S(1)} fusion(bf16[1,2,768,1536]{3,2,0,1:T(8,128)(2,1)} %all_to_all.100, f32[]{:T(128)S(6)} %add.409), kind=kOutput, calls=%fused_computation.70 | convolution fusion | flops 21747990528 | bytes 7077892 | tf_op jit(solution)/shard_map/kif,kjf->kij/dot_general | solution.py:36
  1152.0 27.9 %convolution_add_fusion = f32[768,3072]{1,0:T(8,128)S(1)} fusion(f32[768,3072]{1,0:T(8,128)} %copy.222, f32[768,3072]{0,1:T(8,128)} %bitcast.345, f32[768,768,1]{1,0,2:T(8,128)S(1)} %fusion.47, f32[768,768]{1,0:T(8,128)} %fusion.89), kind=kOutput, calls=%fused_computation.83 | convolution fusion | flops 21747400704 | bytes 33030144 | tf_op jit(solution)/shard_map/kij,kjf->kif/dot_general | solution.py:40
  1179.9 24.3 %fusion.231 = f32[768,768]{1,0:T(8,128)S(1)} fusion(f32[768,3072]{1,0:T(8,128)S(1)} %convolution_add_fusion), kind=kOutput, calls=%fused_computation.359 | convolution fusion | flops 21743271936 | bytes 11796480 | tf_op jit(solution)/shard_map/kif,kjf->kij/dot_general | solution.py:36
  1210.2 24.3 %multiply_add_fusion.2 = f32[768,3072]{1,0:T(8,128)S(1)} fusion(f32[768,3072]{1,0:T(8,128)S(1)} %convolution_add_fusion, f32[768,768]{1,0:T(8,128)S(1)} %fusion.232, f32[768,768]{1,0:T(8,128)S(1)} %fusion.231), kind=kOutput, calls=%fused_computation.77 | convolution fusion | flops 21749760000 | bytes 23592960 | tf_op jit(solution)/shard_map/kij,kjf->kif/dot_general | solution.py:40
  1234.5 23.9 %fusion.233 = f32[768,768]{1,0:T(8,128)S(1)} fusion(f32[768,3072]{1,0:T(8,128)S(1)} %multiply_add_fusion.2), kind=kOutput, calls=%fused_computation.361 | convolution fusion | flops 21743271936 | bytes 11796480 | tf_op jit(solution)/shard_map/kif,kjf->kij/dot_general | solution.py:36
  1264.4 24.3 %multiply_add_fusion.1 = f32[768,3072]{1,0:T(8,128)S(1)} fusion(f32[768,3072]{1,0:T(8,128)S(1)} %multiply_add_fusion.2, f32[768,768]{1,0:T(8,128)S(1)} %fusion.234, f32[768,768]{1,0:T(8,128)S(1)} %fusion.233), kind=kOutput, calls=%fused_computation.76 | convolution fusion | flops 21749760000 | bytes 23592960 | tf_op jit(solution)/shard_map/kij,kjf->kif/dot_general | solution.py:40
  1288.7 23.9 %fusion.235 = f32[768,768]{1,0:T(8,128)S(1)} fusion(f32[768,3072]{1,0:T(8,128)S(1)} %multiply_add_fusion.1), kind=kOutput, calls=%fused_computation.363 | convolution fusion | flops 21743271936 | bytes 11796480 | tf_op jit(solution)/shard_map/kif,kjf->kij/dot_general | solution.py:36
  1318.6 24.3 %multiply_add_fusion = f32[768,3072]{1,0:T(8,128)S(1)} fusion(f32[768,3072]{1,0:T(8,128)S(1)} %multiply_add_fusion.1, f32[768,768]{1,0:T(8,128)S(1)} %fusion.236, f32[768,768]{1,0:T(8,128)S(1)} %fusion.235), kind=kOutput, calls=%fused_computation.75 | convolution fusion | flops 21749760000 | bytes 23592960 | tf_op jit(solution)/shard_map/kij,kjf->kif/dot_general | solution.py:40
  1342.9 23.7 %fusion.237 = f32[768,768]{1,0:T(8,128)S(1)} fusion(f32[768,3072]{1,0:T(8,128)S(1)} %multiply_add_fusion), kind=kOutput, calls=%fused_computation.365 | convolution fusion | flops 21743271936 | bytes 11796480 | tf_op jit(solution)/shard_map/kif,kjf->kij/dot_general | solution.py:36
  1372.6 23.7 %fusion.70 = bf16[1,1,768,3072]{3,2,1,0:T(8,128)(2,1)S(1)} fusion(f32[768,3072]{1,0:T(8,128)S(1)} %multiply_add_fusion, f32[768,768]{1,0:T(8,128)S(1)} %fusion.238, f32[768,768]{1,0:T(8,128)S(1)} %fusion.237), kind=kOutput, calls=%fused_computation.120 | convolution fusion | flops 21752119296 | bytes 18874368 | tf_op jit(solution)/shard_map/kij,kjf->kif/dot_general | solution.py:40
  1396.3 44.0 %copy.252 = bf16[1,1,768,3072]{3,1,0,2:T(2,128)(2,1)} copy(bf16[1,1,768,3072]{3,2,1,0:T(8,128)(2,1)S(1)} %fusion.70) | data formatting | bytes 9437184 | tf_op jit(solution)/shard_map/convert_element_type | solution.py:333
  1440.8 29.0 %reduce.22 = bf16[768,3072]{1,0:T(8,128)(2,1)} reduce(bf16[768,1,1,3072]{3,2,1,0:T(2,128)(2,1)} %bitcast.342, bf16[]{:T(256)} %broadcast.661), dimensions={1,2}, to_apply=%bitcast.289.reduce_sub_computation | reduce | bytes 9437186
  1510.8 76.8 %all-to-all-done.8 = bf16[4,2,294912]{2,1,0:T(2,128)(2,1)} async-done(((bf16[4,2,294912]{2,1,0:T(2,128)(2,1)}), bf16[4,2,294912]{2,1,0:T(2,128)(2,1)}, u32[]{:S(2)}, u32[]{:S(2)}) %all-to-all-start.8) | async-done | bytes 4718624 | tf_op jit(solution)/shard_map/all_to_all | solution.py:332
  (417 shorter events, 832.8 us)
Async XLA Ops:
  8.0 71.1 %all-reduce.6.cloned.1.call-start = ((), (), s32[]{:S(2)}) async-start(), calls=%async_computation.14 | async-start | bytes 6291456 | tf_op jit(solution)/shard_map/psum | solution.py:164
  52.9 95.2 %all-gather.5.cloned.1.call-start = ((), (), s32[]{:S(2)}) async-start(), calls=%async_computation.15 | async-start | bytes 5898240 | tf_op jit(solution)/shard_map/all_gather | solution.py:87
  56.0 181.9 %all-gather.7.cloned.1.call-start = ((), (), s32[]{:S(2)}) async-start(), calls=%async_computation.16 | async-start | bytes 5898240 | tf_op jit(solution)/shard_map/all_gather | solution.py:88
  58.9 212.1 %reduce-scatter.13.cloned.1.call-start = ((), (), s32[]{:S(2)}) async-start(), calls=%async_computation.22 | async-start | bytes 4718592
  261.5 54.0 %all-gather.9.cloned.1.call-start = ((), (), s32[]{:S(2)}) async-start(), calls=%async_computation.17 | async-start | bytes 4718592 | tf_op jit(solution)/shard_map/all_gather | solution.py:103
  303.7 126.6 %reduce-scatter.15.cloned.1.call-start = ((), (), s32[]{:S(2)}) async-start(), calls=%async_computation.23 | async-start | bytes 4718592
  307.6 189.3 %copy-start.26 = (f32[1024,8]{0,1:T(8,128)}, f32[1024,8]{0,1:T(8,128)S(1)}, u32[]{:S(2)}) copy-start(f32[1024,8]{0,1:T(8,128)S(1)} %get-tuple-element.416) | copy-start | bytes 98308
  307.6 189.3 %copy-start.35 = (f32[1024]{0:T(1024)}, f32[1024]{0:T(1024)S(1)}, u32[]{:S(2)}) copy-start(f32[1024]{0:T(1024)S(1)} %get-tuple-element.415) | copy-start | bytes 12292
  307.7 189.3 %copy-start.37 = (f32[1024]{0:T(1024)}, f32[1024]{0:T(1024)S(1)}, u32[]{:S(2)}) copy-start(f32[1024]{0:T(1024)S(1)} %fusion.172) | copy-start | bytes 12292
  329.5 167.5 %copy-start.41 = (f32[1024]{0:T(1024)}, f32[1024]{0:T(1024)S(1)}, u32[]{:S(2)}) copy-start(f32[1024]{0:T(1024)S(1)} %fusion.77) | copy-start | bytes 12292
  337.8 43.6 %slice-start.5 = ((s8[4718592]{0:T(1024)(128)(4,1)}), s8[4194304]{0:T(1024)(128)(4,1)S(1)}, s32[]{:S(2)}) async-start(s8[4718592]{0:T(1024)(128)(4,1)} %bitcast.385), calls=%async_computation.30 | async-start | bytes 8388608
  340.0 41.3 %slice-start.6 = ((s8[4718592]{0:T(1024)(128)(4,1)}), s8[524288]{0:T(1024)(128)(4,1)S(1)}, s32[]{:S(2)}) async-start(s8[4718592]{0:T(1024)(128)(4,1)} %bitcast.385), calls=%async_computation.31 | async-start | bytes 1048576
  419.7 65.6 %all-gather.11.cloned.1.call-start = ((), (), s32[]{:S(2)}) async-start(), calls=%async_computation.18 | async-start | bytes 4718592 | tf_op jit(solution)/shard_map/all_gather | solution.py:103
  462.9 139.8 %reduce-scatter.11.cloned.1.call-start = ((), (), s32[]{:S(2)}) async-start(), calls=%async_computation.21 | async-start | bytes 5898240 | tf_op jit(solution)/shard_map/reduce_scatter | solution.py:290
  474.9 186.2 %reduce-scatter.9.cloned.1.call-start = ((), (), s32[]{:S(2)}) async-start(), calls=%async_computation.20 | async-start | bytes 5898240 | tf_op jit(solution)/shard_map/reduce_scatter | solution.py:287
  475.2 21.8 %copy-start.53 = (f32[1024]{0:T(1024)}, f32[1024]{0:T(1024)S(1)}, u32[]{:S(2)}) copy-start(f32[1024]{0:T(1024)S(1)} %neg.6) | copy-start | bytes 12292
  485.3 185.8 %all-reduce.8.cloned.1.call-start = ((), (), s32[]{:S(2)}) async-start(), calls=%async_computation.19 | async-start | bytes 3145728 | tf_op jit(solution)/shard_map/psum | solution.py:276
  583.3 236.5 %all-reduce.10.cloned.1.call-start = ((), (), s32[]{:S(2)}) async-start(), calls=%async_computation.24 | async-start | bytes 9437184 | tf_op jit(solution)/shard_map/psum | solution.py:283
  674.7 148.0 %copy-start.10 = (f32[3,768,384]{1,2,0:T(8,128)S(1)}, f32[3,768,384]{1,2,0:T(8,128)}, u32[]{:S(2)}) copy-start(f32[3,768,384]{1,2,0:T(8,128)} %copy.210) | copy-start | bytes 10616836
  836.0 219.1 %all-to-all-start.6 = ((bf16[4,2,192,1536]{3,2,1,0:T(8,128)(2,1)}), bf16[4,2,192,1536]{3,2,1,0:T(8,128)(2,1)}, u32[]{:S(2)}, u32[]{:S(2)}) async-start(bf16[4,2,192,1536]{3,2,1,0:T(8,128)(2,1)} %bitcast.347), calls=%async_computation.8 | async-start | bytes 9437184 | tf_op jit(solution)/shard_map/all_to_all | solution.py:324
  1066.3 410.2 %all-to-all-start.5 = ((bf16[2,768,768]{1,0,2:T(2,128)(2,1)}), bf16[2,768,768]{1,0,2:T(2,128)(2,1)}, u32[]{:S(2)}, u32[]{:S(2)}) async-start(bf16[2,768,768]{1,0,2:T(2,128)(2,1)} %copy.212), calls=%async_computation.5 | async-start | bytes 4718592 | tf_op jit(solution)/shard_map/all_to_all | solution.py:302
  1071.4 39.3 %slice-start = ((s8[4718592]{0:T(1024)(128)(4,1)}), s8[524288]{0:T(1024)(128)(4,1)S(1)}, s32[]{:S(2)}) async-start(s8[4718592]{0:T(1024)(128)(4,1)} %bitcast.338), calls=%async_computation.25 | async-start | bytes 1048576
  1077.6 33.2 %slice-start.1 = ((s8[4718592]{0:T(1024)(128)(4,1)}), s8[4194304]{0:T(1024)(128)(4,1)S(1)}, s32[]{:S(2)}) async-start(s8[4718592]{0:T(1024)(128)(4,1)} %bitcast.338), calls=%async_computation.26 | async-start | bytes 8388608
  1476.6 111.1 %all-to-all-start.8 = ((bf16[4,2,294912]{2,1,0:T(2,128)(2,1)}), bf16[4,2,294912]{2,1,0:T(2,128)(2,1)}, u32[]{:S(2)}, u32[]{:S(2)}) async-start(bf16[4,2,294912]{2,1,0:T(2,128)(2,1)} %reshape.688), calls=%async_computation.10 | async-start | bytes 9437184 | tf_op jit(solution)/shard_map/all_to_all | solution.py:332
  (68 other events, 397.1 us)
Sparse Core Ops, SparseCore 0:
  53.0 26.0 all-reduce.5
  261.6 9.3 reduce-scatter.12
  303.8 11.7 all-gather.8
  419.8 10.3 reduce-scatter.14
  463.0 11.7 all-gather.10
  583.4 20.2 all-reduce.7
  610.1 209.6 all-reduce.9
Sparse Core Ops, SparseCore 1:
  56.1 91.9 all-gather.4
  150.2 87.7 all-gather.6
  475.0 84.9 reduce-scatter.10
  562.3 98.7 reduce-scatter.8
where the time goes:
time: 1680 us; the launch traced here: 1670 us
  matrix products  627 us (37%)
  waiting for transfers between devices  328 us (20%)
  local copies, waits for them, and re-layouts  269 us (16%)
  blocking collectives  246 us (15%)
  other arithmetic  166 us (10%)
  between operations  18.8 us (1%)
  starting transfers between devices  16.9 us (1%)
    dot_general x15, matrix products, newton_whole(): jnp.einsum('kij,kjf->kif', polynomial, orthogonal, precision=PRECISE)  190 us
    dot_general x15, matrix products, newton_whole(): jnp.einsum('kif,kjf->kij', orthogonal, orthogonal, precision=PRECISE)  188 us
    dot_general x15, matrix products, newton_whole(): jnp.einsum('kij,kjl->kil', gram_matrix, gram_matrix, precision=PRECISE)  93.8 us
    unnamed x156, local copies, waits for them, and re-layouts  85 us
    all_to_all x2, blocking collectives, dispatch(): lax.all_to_all(grid_rows, 'expert', split_axis=1, concat_axis=1, tiled=True)  81.9 us
    all_gather x1, waiting for transfers between devices, body(): lax.all_gather(w_out.astype(jnp.bfloat16), 'dp', axis=1, tiled=True)  79.1 us
    psum x1, blocking collectives, body(): lax.psum((attention_gradient, grad_proj, grad_router, gain_grads, bias_gr...  78.9 us
    all_to_all x1, waiting for transfers between devices, body(): lax.all_to_all(whole_ortho.reshape(1, 1, model_width, tensor_count * col_...  76.8 us
  transfers between devices with their start and end apart: 14, of which 9 were waited for; matrix products, arithmetic and copies ran while one was open for 50% of the time, Pallas kernels for 0%

commit v1 on v0

--- a/solution.py
+++ b/solution.py
@@ -39,6 +39,38 @@
         )
         orthogonal = COEF_A * orthogonal + jnp.einsum(
             "kij,kjf->kif", polynomial, orthogonal, precision=PRECISE
+        )
+    return orthogonal
+
+
+def product(spec, left, right):
+    return jnp.einsum(
+        spec,
+        left.astype(jnp.bfloat16),
+        right.astype(jnp.bfloat16),
+        preferred_element_type=jnp.float32,
+    )
+
+
+def mean_diagonal(matrices, identity):
+    return jnp.sum(matrices * identity, axis=(-2, -1), keepdims=True) / identity.shape[-1]
+
+
+def newton_low(update):
+    frobenius = jnp.sqrt(jnp.sum(update * update, axis=(-2, -1), keepdims=True))
+    orthogonal = update / (frobenius + 1e-07)
+    identity = jnp.eye(update.shape[-2], dtype=jnp.float32)
+    for iteration in range(NS_STEPS):
+        gram_matrix = product("kif,kjf->kij", orthogonal, orthogonal)
+        level = mean_diagonal(gram_matrix, identity)
+        rest = gram_matrix - level * identity
+        polynomial_rest = (COEF_B + 2.0 * COEF_C * level) * rest + COEF_C * product(
+            "kij,kjl->kil", rest, rest
+        )
+        shift = mean_diagonal(polynomial_rest, identity)
+        factor = COEF_A + COEF_B * level + COEF_C * level * level + shift
+        orthogonal = factor * orthogonal + product(
+            "kij,kjf->kif", polynomial_rest - shift * identity, orthogonal
         )
     return orthogonal
 
@@ -280,9 +312,15 @@
     input_grad = hidden_grad + input_norm_grad
     gain_grads = jnp.stack([grad_gain_one, grad_gain_two])
     bias_grads = jnp.stack([bias_pair[0], bias_pair[1], grad_bias_out])
-    attention_gradient, grad_proj, grad_router, gain_grads, bias_grads = lax.psum(
-        (attention_gradient, grad_proj, grad_router, gain_grads, bias_grads), ("expert", "dp")
-    )
+    dense_gradient = jnp.concatenate([attention_gradient, grad_proj.T[None]], axis=0)
+    dense_gradient = lax.psum(dense_gradient.astype(jnp.bfloat16), ("expert", "dp")).astype(
+        jnp.float32
+    )
+    attention_gradient, grad_proj = (dense_gradient[:3], dense_gradient[3].T)
+    small_grads = lax.psum(
+        jnp.concatenate([gain_grads, bias_grads, grad_router.T], axis=0), ("expert", "dp")
+    )
+    gain_grads, bias_grads, grad_router = (small_grads[:2], small_grads[2:5], small_grads[5:].T)
     grad_in_w, grad_out_w = (
         lax.psum_scatter(
             grad_in_w.astype(jnp.bfloat16), "dp", scatter_dimension=1, tiled=True
@@ -298,9 +336,11 @@
     proj_moment_new = MOMENT * proj_moment + grad_proj
     proj_update = grad_proj + MOMENT * proj_moment_new
     dense_stack = jnp.concatenate([attn_update, proj_update.T[None]], axis=0)
-    owned = lax.all_to_all(dense_stack, "tensor", split_axis=0, concat_axis=2, tiled=True)
+    owned = lax.all_to_all(
+        dense_stack.astype(jnp.bfloat16), "tensor", split_axis=0, concat_axis=2, tiled=True
+    ).astype(jnp.float32)
     settled = lax.all_to_all(
-        newton_whole(owned).astype(jnp.bfloat16), "tensor", split_axis=2, concat_axis=0, tiled=True
+        newton_low(owned).astype(jnp.bfloat16), "tensor", split_axis=2, concat_axis=0, tiled=True
     ).astype(jnp.float32)
     dense_factor = math.sqrt(model_width)
     new_attn = w_attn - RATE_ATTN * dense_factor * settled[:3]
@@ -327,21 +367,20 @@
         concat_axis=3,
         tiled=True,
     ).astype(padded.dtype)
-    whole_ortho = newton_whole(whole_matrix.reshape(1, model_width, tensor_count * col_part))
-    returned = lax.all_to_all(
-        lax.all_to_all(
-            whole_ortho.reshape(1, 1, model_width, tensor_count * col_part).astype(jnp.bfloat16),
-            "dp",
-            split_axis=2,
-            concat_axis=0,
-            tiled=True,
-        ),
-        "tensor",
-        split_axis=3,
-        concat_axis=1,
-        tiled=True,
+    whole_ortho = newton_low(whole_matrix.reshape(1, model_width, tensor_count * col_part))
+    ortho_low = whole_ortho.astype(jnp.bfloat16).reshape(
+        data_count, row_part, tensor_count * col_part
+    )
+    column_parts = jnp.stack(
+        [ortho_low[:, :, t * col_part : (t + 1) * col_part] for t in range(tensor_count)]
+    )
+    own_columns = lax.all_to_all(
+        column_parts, "tensor", split_axis=0, concat_axis=0, tiled=True
+    )
+    returned = lax.all_to_all(own_columns, "dp", split_axis=1, concat_axis=1, tiled=True)
+    expert_ortho = jnp.stack(
+        [returned[m % tensor_count, m // tensor_count] for m in range(stack_count)]
     ).astype(jnp.float32)
-    expert_ortho = returned.reshape(slot_total, row_part, col_part)[:stack_count]
     expert_factor = math.sqrt(max(model_width, FF))
     new_in = w_in - RATE_IN * expert_factor * expert_ortho[:expert_local]
     new_out = w_out - RATE_OUT * expert_factor * expert_ortho[expert_local:]

time: 1680 us -> 1260 us (0.75)
  matrix products: 627 us -> 369 us
  local copies, waits for them, and re-layouts: 269 us -> 183 us
  waiting for transfers between devices: 328 us -> 272 us
  other arithmetic: 166 us -> 131 us
  between operations: 18.8 us -> 38.4 us
    dot_general x0 -> x30, matrix products: none -> 205 us  [product(): jnp.einsum(spec, left.astype(jnp.bfloat16), right.astype(jnp.bfloat16), p...]
    dot_general x15 -> x5, matrix products: 190 us -> 1.49 us  [newton_whole(): jnp.einsum('kij,kjf->kif', polynomial, orthogonal, precision=PRECISE)]
    dot_general x15 -> x5, matrix products: 188 us -> 0.68 us  [newton_whole(): jnp.einsum('kif,kjf->kij', orthogonal, orthogonal, precision=PRECISE)]
    dot_general x15 -> x5, matrix products: 93.8 us -> 0.79 us  [newton_whole(): jnp.einsum('kij,kjl->kil', gram_matrix, gram_matrix, precision=PRECISE)]
    psum x1, waiting for transfers between devices: 62 us -> 29.3 us  [body(): lax.psum(dense_gradient.astype(jnp.bfloat16), ('expert', 'dp'))]
    convert_element_type x4 -> x5, local copies, waits for them, and re-layouts: 61.5 us -> 29.6 us  [the longest x2 15.7 us: body(): owned = lax.all_to_all(dense_stack.astype(jnp.bfloat16), 'tensor', split_...]
    all_to_all x4 -> x1, local copies, waits for them, and re-layouts: 35.8 us -> 4.85 us  [body(): lax.all_to_all(column_parts, 'tensor', split_axis=0, concat_axis=0, tiled...]
    unnamed x7 -> x5, other arithmetic: 29.1 us -> 0.08 us
  transfers between devices with their start and end apart: 14 -> 14, of which waited for: 9 -> 9; matrix products, arithmetic and copies ran while one was open for 50% -> 29% of each run, Pallas kernels for 0% -> 0%
where the time goes in v1:
time: 1260 us; the launch traced here: 1250 us
  matrix products  369 us (29%)
  waiting for transfers between devices  272 us (22%)
  blocking collectives  235 us (19%)
  local copies, waits for them, and re-layouts  183 us (15%)
  other arithmetic  131 us (10%)
  between operations  38.4 us (3%)
  starting transfers between devices  16.5 us (1%)
    dot_general x30, matrix products, product(): jnp.einsum(spec, left.astype(jnp.bfloat16), right.astype(jnp.bfloat16), p...  205 us
    all_to_all x2, blocking collectives, dispatch(): lax.all_to_all(grid_rows, 'expert', split_axis=1, concat_axis=1, tiled=True)  81.9 us
    all_gather x1, waiting for transfers between devices, body(): lax.all_gather(w_out.astype(jnp.bfloat16), 'dp', axis=1, tiled=True)  79 us
    psum x1, blocking collectives, body(): lax.psum(jnp.concatenate([gain_grads, bias_grads, grad_router.T], axis=0)...  77.7 us
    all_to_all x1, waiting for transfers between devices, body(): lax.all_to_all(own_columns, 'dp', split_axis=1, concat_axis=1, tiled=True)  76.1 us
    unnamed x172, local copies, waits for them, and re-layouts  62.7 us
    all_to_all x2, blocking collectives, give_back(): lax.all_to_all(summed, 'expert', split_axis=1, concat_axis=1, tiled=True)  49.8 us
    reduce_scatter x1, waiting for transfers between devices, body(): lax.psum_scatter(grad_in_w.astype(jnp.bfloat16), 'dp', scatter_dimension=...  31.9 us
  transfers between devices with their start and end apart: 14, of which 9 were waited for; matrix products, arithmetic and copies ran while one was open for 29% of the time, Pallas kernels for 0%

profile of v1, /device:TPU:0, one launch (start us, length us, event | category | flops | bytes accessed | tf_op | source)
XLA Modules:
  0.0 1245.5 jit_solution(8836951574048408624)
XLA Ops:
  24.6 29.4 %while.27 = (s32[]{:T(128)}, bf16[2,512,6,64]{1,3,2,0:T(8,128)(2,1)S(1)}, f32[2,6,512]{2,1,0:T(8,128)}, s32[2,512]{1,0:T(2,128)}, s32[1024]{0:T(1024)}, /*index=...) while((s32[]{:T(128)}, ...), condition=%wide.region_7.8_spmd, body=%wide.region_3.7_spmd.sunk | while | flops 850076672 | bytes 42375784 | solution.py:192
  67.0 17.3 %all-reduce.4.cloned.1.call-done = f32[1024,768]{1,0:T(8,128)} async-done(((f32[1024,768]{1,0:T(8,128)}), f32[1024,768]{1,0:T(8,128)}) %all-reduce.4.cloned.1.call-update) | async-done | bytes 3145744 | tf_op jit(solution)/shard_map/psum | solution.py:196
  99.4 40.8 %all_to_all.75 = bf16[2,4,256,768]{3,2,0,1:T(8,128)(2,1)S(1)} all-to-all(bf16[2,4,256,768]{3,2,0,1:T(8,128)(2,1)S(1)} %copy.187), channel_id=1, replica_groups=mesh['expert'=4,'dp'=4,'tensor'=2] {'expert'}, dimensions={1} | all-to-all | bytes 6291456 | tf_op jit(solution)/shard_map/all_to_all | solution.py:144
  142.1 11.1 all-gather.5.cloned.1.call-done
  153.2 10.9 fusion.251
  164.0 79.0 %all-gather.7.cloned.1.call-done = bf16[2,768,1536]{2,1,0:T(8,128)(2,1)} async-done(((bf16[2,192,1536]{2,1,0:T(8,128)(2,1)}), bf16[2,768,1536]{2,1,0:T(8,128)(2,1)}) %all-gather.7.cloned.1.call-update) | async-done | bytes 4718608 | tf_op jit(solution)/shard_map/all_gather | solution.py:120
  243.0 11.3 convolution_convert_fusion.3
  283.8 24.9 %all_to_all.76 = bf16[2,4,256,384]{3,2,0,1:T(8,128)(2,1)} all-to-all(bf16[2,4,256,384]{3,2,0,1:T(8,128)(2,1)} %copy.189), channel_id=1, replica_groups=mesh['expert'=4,'dp'=4,'tensor'=2] {'expert'}, dimensions={1} | all-to-all | bytes 3145728 | tf_op jit(solution)/shard_map/all_to_all | solution.py:152
  345.2 41.1 %all_to_all.77 = bf16[2,4,256,768]{3,2,0,1:T(8,128)(2,1)S(1)} all-to-all(bf16[2,4,256,768]{3,2,0,1:T(8,128)(2,1)S(1)} %copy.191), channel_id=1, replica_groups=mesh['expert'=4,'dp'=4,'tensor'=2] {'expert'}, dimensions={1} | all-to-all | bytes 6291456 | tf_op jit(solution)/shard_map/all_to_all | solution.py:144
  386.5 16.8 %fusion.45 = bf16[2,1024,1536]{2,1,0:T(8,128)(2,1)} fusion(f32[2,1024,1536]{2,1,0:T(8,128)} %fusion.251, bf16[2,1024,768]{2,1,0:T(8,128)(2,1)S(1)} %bitcast.345, bf16[2,768,1536]{2,1,0:T(8,128)(2,1)S(1)} %bitcast.368), kind=kOutput, calls=%fused_computation.65 | convolution fusion | flops 4894752768 | bytes 26738688 | tf_op jit(solution)/shard_map/jrd,jdf->jrf/dot_general | solution.py:221
  424.9 10.5 reduce-scatter.15.cloned.1.call-done
  443.1 24.9 %all_to_all.78 = bf16[2,4,256,384]{3,2,0,1:T(8,128)(2,1)} all-to-all(bf16[2,4,256,384]{3,2,0,1:T(8,128)(2,1)} %copy.193), channel_id=1, replica_groups=mesh['expert'=4,'dp'=4,'tensor'=2] {'expert'}, dimensions={1} | all-to-all | bytes 3145728 | tf_op jit(solution)/shard_map/all_to_all | solution.py:152
  468.1 11.8 convolution_convert_fusion
  519.2 67.4 %while.28 = (s32[]{:T(128)}, f32[1024,6,64]{0,2,1:T(8,128)}, f32[1024,6,64]{0,2,1:T(8,128)}, bf16[2,512,6,64]{1,3,2,0:T(8,128)(2,1)}, bf16[2,512,6,64]{1,3,2,0:T...) while((s32[]{:T(128)}, f32[1024,6,64]{0,2,1:T(8,128)}, ...), condition=%wide.region_25.26_spmd.clone, body=%wide.region_23.25_spmd.clone.sunk | while | flops 2063332352 | bytes 217287984 | solution.py:277
  621.5 31.9 %reduce-scatter.9.cloned.1.call-done = bf16[2,192,1536]{2,1,0:T(8,128)(2,1)} async-done(((bf16[2,768,1536]{2,1,0:T(8,128)(2,1)}), bf16[2,192,1536]{2,1,0:T(8,128)(2,1)}) %reduce-scatter.9.cloned.1.call-update) | async-done | bytes 1179664 | tf_op jit(solution)/shard_map/reduce_scatter | solution.py:325
  667.1 77.7 %psum.38 = f32[13,768]{1,0:T(8,128)S(1)} all-reduce(f32[13,768]{1,0:T(8,128)S(1)} %concatenate.16), channel_id=1, replica_groups=mesh['expert'=4,'dp'=4,'tensor'=2] {'expert','dp'}, use_global_device_ids=true, to_apply=%region_34.35 | all-reduce | flops 9984 | bytes 79872 | tf_op jit(solution)/shard_map/psum | solution.py:320
  746.6 29.3 %all-reduce.8.cloned.1.call-done = bf16[4,768,384]{1,2,0:T(8,128)(2,1)} async-done(((bf16[4,768,384]{1,2,0:T(8,128)(2,1)}), bf16[4,768,384]{1,2,0:T(8,128)(2,1)}) %all-reduce.8.cloned.1.call-update) | async-done | bytes 2359312 | tf_op jit(solution)/shard_map/psum | solution.py:316
  824.8 10.3 multiply_reduce_fusion.9
  897.6 10.2 multiply_reduce_fusion.1
  1013.2 10.5 multiply_add_fusion.2
  1038.4 10.7 multiply_add_fusion.1
  1063.9 10.5 multiply_add_fusion
  1089.1 10.8 add_convert_fusion
  1154.0 76.1 %all-to-all-done.9 = bf16[2,4,192,1536]{3,2,0,1:T(8,128)(2,1)} async-done(((bf16[2,4,192,1536]{3,2,0,1:T(8,128)(2,1)}), bf16[2,4,192,1536]{3,2,0,1:T(8,128)(2,1)}, u32[]{:S(2)}, u32[]{:S(2)}) %all-to-all-start.9) | async-done | bytes 4718624 | tf_op jit(solution)/shard_map/all_to_all | solution.py:380
  (449 shorter events, 628.2 us)
Async XLA Ops:
  8.0 76.2 %all-reduce.4.cloned.1.call-start = ((), (), s32[]{:S(2)}) async-start(), calls=%async_computation.14 | async-start | bytes 6291456 | tf_op jit(solution)/shard_map/psum | solution.py:196
  58.0 95.2 %all-gather.5.cloned.1.call-start = ((), (), s32[]{:S(2)}) async-start(), calls=%async_computation.15 | async-start | bytes 5898240 | tf_op jit(solution)/shard_map/all_gather | solution.py:119
  61.1 181.9 %all-gather.7.cloned.1.call-start = ((), (), s32[]{:S(2)}) async-start(), calls=%async_computation.16 | async-start | bytes 5898240 | tf_op jit(solution)/shard_map/all_gather | solution.py:120
  64.0 212.1 %reduce-scatter.13.cloned.1.call-start = ((), (), s32[]{:S(2)}) async-start(), calls=%async_computation.23 | async-start | bytes 4718592
  266.6 54.1 %all-gather.9.cloned.1.call-start = ((), (), s32[]{:S(2)}) async-start(), calls=%async_computation.17 | async-start | bytes 4718592 | tf_op jit(solution)/shard_map/all_gather | solution.py:135
  308.7 126.6 %reduce-scatter.15.cloned.1.call-start = ((), (), s32[]{:S(2)}) async-start(), calls=%async_computation.24 | async-start | bytes 4718592
  312.7 189.3 %copy-start.37 = (f32[1024,8]{0,1:T(8,128)}, f32[1024,8]{0,1:T(8,128)S(1)}, u32[]{:S(2)}) copy-start(f32[1024,8]{0,1:T(8,128)S(1)} %get-tuple-element.439) | copy-start | bytes 98308
  312.7 189.3 %copy-start.48 = (f32[1024]{0:T(1024)}, f32[1024]{0:T(1024)S(1)}, u32[]{:S(2)}) copy-start(f32[1024]{0:T(1024)S(1)} %get-tuple-element.438) | copy-start | bytes 12292
  312.7 189.3 %copy-start.50 = (f32[1024]{0:T(1024)}, f32[1024]{0:T(1024)S(1)}, u32[]{:S(2)}) copy-start(f32[1024]{0:T(1024)S(1)} %fusion.210) | copy-start | bytes 12292
  334.6 167.4 %copy-start.53 = (f32[1024]{0:T(1024)}, f32[1024]{0:T(1024)S(1)}, u32[]{:S(2)}) copy-start(f32[1024]{0:T(1024)S(1)} %fusion.61) | copy-start | bytes 12292
  342.9 43.6 %slice-start.3 = ((s8[4718592]{0:T(1024)(128)(4,1)}), s8[4194304]{0:T(1024)(128)(4,1)S(1)}, s32[]{:S(2)}) async-start(s8[4718592]{0:T(1024)(128)(4,1)} %bitcast.367), calls=%async_computation.28 | async-start | bytes 8388608
  345.2 41.3 %slice-start.4 = ((s8[4718592]{0:T(1024)(128)(4,1)}), s8[524288]{0:T(1024)(128)(4,1)S(1)}, s32[]{:S(2)}) async-start(s8[4718592]{0:T(1024)(128)(4,1)} %bitcast.367), calls=%async_computation.29 | async-start | bytes 1048576
  386.2 17.0 %slice-start.1 = ((s8[4718592]{0:T(1024)(128)(4,1)}), s8[4194304]{0:T(1024)(128)(4,1)S(1)}, s32[]{:S(2)}) async-start(s8[4718592]{0:T(1024)(128)(4,1)} %bitcast.365), calls=%async_computation.26 | async-start | bytes 8388608
  424.8 65.5 %all-gather.11.cloned.1.call-start = ((), (), s32[]{:S(2)}) async-start(), calls=%async_computation.18 | async-start | bytes 4718592 | tf_op jit(solution)/shard_map/all_gather | solution.py:135
  468.0 148.8 %reduce-scatter.11.cloned.1.call-start = ((), (), s32[]{:S(2)}) async-start(), calls=%async_computation.22 | async-start | bytes 5898240 | tf_op jit(solution)/shard_map/reduce_scatter | solution.py:328
  479.9 173.5 %reduce-scatter.9.cloned.1.call-start = ((), (), s32[]{:S(2)}) async-start(), calls=%async_computation.21 | async-start | bytes 5898240 | tf_op jit(solution)/shard_map/reduce_scatter | solution.py:325
  480.2 21.8 %copy-start.64 = (f32[1024]{0:T(1024)}, f32[1024]{0:T(1024)S(1)}, u32[]{:S(2)}) copy-start(f32[1024]{0:T(1024)S(1)} %neg.6) | copy-start | bytes 12292
  490.3 172.6 %all-reduce.6.cloned.1.call-start = ((), (), s32[]{:S(2)}) async-start(), calls=%async_computation.19 | async-start | bytes 3145728 | tf_op jit(solution)/shard_map/psum | solution.py:308
  600.7 175.2 %all-reduce.8.cloned.1.call-start = ((), (), s32[]{:S(2)}) async-start(), calls=%async_computation.20 | async-start | bytes 4718592 | tf_op jit(solution)/shard_map/psum | solution.py:316
  660.0 84.7 %copy-start.69 = (f32[768,8]{0,1:T(8,128)S(1)}, f32[768,8]{0,1:T(8,128)}, u32[]{:S(2)}) copy-start(f32[768,8]{0,1:T(8,128)} %param.37) | copy-start | bytes 73732
  744.7 33.4 %copy-start.42 = (f32[13,768]{1,0:T(8,128)}, f32[13,768]{1,0:T(8,128)S(1)}, u32[]{:S(2)}) copy-start(f32[13,768]{1,0:T(8,128)S(1)} %psum.38) | copy-start | bytes 119812
  789.1 131.4 %all-to-all-start.6 = ((bf16[4,2,192,1536]{3,2,1,0:T(8,128)(2,1)}), bf16[4,2,192,1536]{3,2,1,0:T(8,128)(2,1)}, u32[]{:S(2)}, u32[]{:S(2)}) async-start(bf16[4,2,192,1536]{3,2,1,0:T(8,128)(2,1)} %bitcast.327), calls=%async_computation.8 | async-start | bytes 9437184 | tf_op jit(solution)/shard_map/all_to_all | solution.py:364
  1109.3 9.9 all-to-all-start.5
  1119.2 110.9 %all-to-all-start.9 = ((bf16[2,4,192,1536]{3,2,0,1:T(8,128)(2,1)}), bf16[2,4,192,1536]{3,2,0,1:T(8,128)(2,1)}, u32[]{:S(2)}, u32[]{:S(2)}) async-start(bf16[2,4,192,1536]{3,2,0,1:T(8,128)(2,1)} %copy.216), calls=%async_computation.11 | async-start | bytes 9437184 | tf_op jit(solution)/shard_map/all_to_all | solution.py:380
  (81 other events, 449.9 us)
Sparse Core Ops, SparseCore 0:
  58.1 26.0 all-reduce.3
  266.7 9.3 reduce-scatter.12
  308.8 11.7 all-gather.8
  424.9 10.3 reduce-scatter.14
  468.1 11.7 all-gather.10
  600.8 20.3 all-reduce.5
  627.4 148.4 all-reduce.7
Sparse Core Ops, SparseCore 1:
  61.2 91.9 all-gather.4
  155.3 87.7 all-gather.6
  480.0 84.9 reduce-scatter.10
  567.3 86.0 reduce-scatter.8
